TPU v7x, 32 devices: a whole 2x2x4 slice. The times are simulated.
32 devices in a mesh: face: 8 (over y, x, core), tile: 4 (over z).
Axes of the slice: x: 2, y: 2, z: 4, core: 2. Of those that a mesh axis runs over, the one named last changes fastest.
Arguments:
- state: float32 [32, 4, 2, 128, 128], P(('face', 'tile')), may hold values from -3 to 3
- forcing: float32 [32, 2, 4, 128, 128], P(('face', 'tile')), may hold values from -3 to 3
- cotangent: float32 [32, 4, 2, 128, 128], P(('face', 'tile')), may hold values from -6 to 6
- neighbour: int32 [32, 4], P(('face', 'tile')), may hold values from -1 to 31, as said below
- rotation: int32 [32, 4], P(('face', 'tile')), may hold values from 0 to 7
- wet: int32 [32], P(('face', 'tile')), may hold values from 0 to 1, as said below
- levels: int32 [32, 128, 128], P(('face', 'tile')), may hold values from 0 to 2
Outputs:
- state_gradient: float32 [32, 4, 2, 128, 128], P(('face', 'tile'))
- forcing_gradient: float32 [32, 2, 4, 128, 128], P(('face', 'tile'))
Inputs may be any that keep to these rules, and one draw needn't show every extreme that they name: The west neighbour of every tile is the tile of the same slot on the device with the same tile index at face index one below (wrapping around the face axis), the east neighbour the one at face index one above; south and north neighbours lie on a device of the same face block or are -1. Every tile on a device of tile index 0 is wet.
All inputs are finite; a program needn't handle non-finite values.
Results may differ from a plain program's by a relative error of at most 0.00005.
Values sent between devices are 32-bit elements; how exact they have to be, the bound alone decides.
A program may use at most 64 MiB of HBM per device.

v0:
```python
import jax
import jax.numpy as jnp
from jax import lax
from jax.sharding import PartitionSpec as P

time_step = 1.0
diffuse_rate = 0.15
viscosity = 0.15
vertical_mix = 0.1
coriolis = 0.3
buoyancy_scale = 0.25
thermal_coef = 1.0
haline_coef = 0.8
drag_rate = 0.05


def with_halo(block, sides, width):
    for axis, dim in sides:
        count = lax.axis_size(axis)
        forward = [(i, i + 1) for i in range(count - 1)]
        forward.append((count - 1, 0))
        backward = [(target, source) for source, target in forward]
        low = lax.ppermute(
            lax.slice_in_dim(block, block.shape[dim] - width, None, axis=dim), axis, forward
        )
        high = lax.ppermute(lax.slice_in_dim(block, 0, width, axis=dim), axis, backward)
        block = jnp.concatenate([low, block, high], axis=dim)
    return block


def edge_strips(field):
    return jnp.stack(
        [field[..., :, 0], field[..., :, -1], field[..., 0, :], field[..., -1, :]], axis=1
    )


def place_halo(field, halos):
    padded = jnp.pad(field, ((0, 0), (0, 0), (0, 0), (1, 1), (1, 1)))
    padded = padded.at[..., 1:-1, 0].set(halos[:, 0])
    padded = padded.at[..., 1:-1, -1].set(halos[:, 1])
    padded = padded.at[..., 0, 1:-1].set(halos[:, 2])
    padded = padded.at[..., -1, 1:-1].set(halos[:, 3])
    return padded


def level_mix(values):
    above = jnp.concatenate([values[:, :1], values[:, :-1]], axis=1)
    below = jnp.concatenate([values[:, 1:], values[:, -1:]], axis=1)
    return above + below - 2.0 * values


def step_tiles(padded, mask, drive):
    centre = padded[..., 1:-1, 1:-1]
    east = padded[..., 1:-1, 2:]
    west = padded[..., 1:-1, :-2]
    north = padded[..., 2:, 1:-1]
    south = padded[..., :-2, 1:-1]
    laplace = east + west + north + south - 4.0 * centre
    grad_x = 0.5 * (east - west)
    grad_y = 0.5 * (north - south)
    theta = centre[:, 0]
    salt = centre[:, 1]
    uvel = centre[:, 2]
    vvel = centre[:, 3]
    dens_x = -thermal_coef * grad_x[:, 0] + haline_coef * grad_x[:, 1]
    dens_y = -thermal_coef * grad_y[:, 0] + haline_coef * grad_y[:, 1]
    new_theta = theta + time_step * (
        -(uvel * grad_x[:, 0] + vvel * grad_y[:, 0])
        + diffuse_rate * laplace[:, 0]
        + vertical_mix * level_mix(theta)
    )
    new_salt = salt + time_step * (
        -(uvel * grad_x[:, 1] + vvel * grad_y[:, 1])
        + diffuse_rate * laplace[:, 1]
        + vertical_mix * level_mix(salt)
    )
    new_u = uvel + time_step * (
        viscosity * laplace[:, 2] + coriolis * vvel - buoyancy_scale * dens_x - drag_rate * uvel
    )
    new_v = vvel + time_step * (
        viscosity * laplace[:, 3] - coriolis * uvel - buoyancy_scale * dens_y - drag_rate * vvel
    )
    result = jnp.stack([new_theta, new_salt, new_u, new_v], axis=1)
    result = result.at[:, :, 0].add(time_step * drive)
    return result * mask[:, None]


def shards(state, forcing, cotangent, neighbour, rotation, wet, levels):
    slot_count = state.shape[0]
    group_size = lax.axis_size("tile")
    face_count = lax.axis_size("face")
    face_index = lax.axis_index("face")
    depth = jnp.arange(state.shape[2], dtype=jnp.int32)[None, :, None, None]
    mask = ((depth < levels[:, None]) & (wet[:, None, None, None] == 1)).astype(jnp.float32)
    valid = neighbour >= 0
    source = jnp.maximum(neighbour, 0)
    device_of = source // slot_count
    slot_of = source % slot_count
    source_face = device_of // group_size
    source_tile = device_of % group_size
    side = rotation % 4
    flip = rotation // 4
    lower_face = (face_index + face_count - 1) % face_count
    block = jnp.where(
        source_face == face_index,
        source_tile,
        jnp.where(source_face == lower_face, group_size, group_size + 1),
    )
    column = (block * slot_count + slot_of) * 4 + side
    total = (group_size + 2) * slot_count * 4
    selector = (
        (column[..., None] == jnp.arange(total, dtype=jnp.int32)) & valid[..., None]
    ).astype(jnp.float32)
    selector = selector.reshape(slot_count * 4, total)
    reverse = (flip == 1)[..., None, None, None]

    def gather_rims(field):
        strips = edge_strips(field)[None]
        grouped = lax.all_gather(strips, "tile", axis=0, tiled=True)
        beside_all = with_halo(strips, (("face", 0),), 1)
        return jnp.concatenate([grouped, beside_all[0:1], beside_all[2:3]], axis=0)

    def assemble(field, candidates):
        flat = candidates.reshape(total, -1)
        chosen = jnp.dot(selector, flat, precision=lax.Precision.HIGHEST)
        chosen = chosen.reshape(slot_count, 4, field.shape[1], field.shape[2], field.shape[3])
        flipped = jnp.where(reverse, chosen[..., ::-1], chosen)
        return place_halo(field, flipped)

    def fill(field):
        return assemble(field, gather_rims(field))

    def fill_back(ct_padded, field):
        cand_shape = (group_size + 2, slot_count, 4, field.shape[1], field.shape[2], field.shape[3])
        blank_cands = jnp.zeros(cand_shape, jnp.float32)
        unused, pull_assemble = jax.vjp(assemble, jnp.zeros_like(field), blank_cands)
        ct_field, ct_cands = pull_assemble(ct_padded)
        back_group = lax.psum_scatter(
            ct_cands[:group_size], "tile", scatter_dimension=0, tiled=True
        )
        back_face = with_halo(ct_cands[group_size:], (("face", 0),), 1)
        ct_strips = back_group[0] + back_face[0] + back_face[3]
        unused_edges, pull_edges = jax.vjp(edge_strips, jnp.zeros_like(field))
        (extra,) = pull_edges(ct_strips)
        return ct_field + extra

    def stepper(padded, drive):
        return step_tiles(padded, mask, drive)

    first = state * mask[:, None]
    padded_first = fill(first)
    second = step_tiles(padded_first, mask, forcing[:, 0])
    padded_second = fill(second)
    unused_a, pull_second = jax.vjp(stepper, padded_second, forcing[:, 1])
    ct_pad_second, ct_drive_second = pull_second(cotangent)
    ct_second = fill_back(ct_pad_second, second)
    unused_b, pull_first = jax.vjp(stepper, padded_first, forcing[:, 0])
    ct_pad_first, ct_drive_first = pull_first(ct_second)
    ct_first = fill_back(ct_pad_first, first)
    state_gradient = ct_first * mask[:, None]
    forcing_gradient = jnp.stack([ct_drive_first, ct_drive_second], axis=1)
    return (state_gradient, forcing_gradient)


def solution(mesh):
    placed = (
        P(("face", "tile"), None, None, None, None),
        P(("face", "tile"), None, None, None, None),
        P(("face", "tile"), None, None, None, None),
        P(("face", "tile"), None),
        P(("face", "tile"), None),
        P(("face", "tile")),
        P(("face", "tile"), None, None),
    )
    return jax.shard_map(
        shards,
        mesh=mesh,
        in_specs=placed,
        out_specs=(
            P(("face", "tile"), None, None, None, None),
            P(("face", "tile"), None, None, None, None),
        ),
        check_vma=False,
    )
```

profile of v0, /device:TPU:0, one launch (start us, length us, event | category | flops | bytes accessed | tf_op | source)
XLA Modules:
  0.0 179.9 jit_solution(9916505326174148500)
XLA Ops:
  7.9 0.9 fusion.43
  8.7 1.1 broadcast_multiply_fusion.1
  10.4 0.5 collective-permute-start
  11.0 2.9 %collective-permute-start.1 = (f32[1,1,4,4,2,128]{5,4,3,2,1,0:T(2,128)S(1)}, f32[1,1,4,4,2,128]{5,4,3,2,1,0:T(2,128)S(1)}, u32[]{:S(2)}, u32[]{:S(2)}) collective-permute-start(f32[1,1,4,4,2,128]{5,4,3,2,1,0:T(2,128)S(1)} %fusion.86), channel_id=1, source_target_pairs={{4,0},{8,4},{12,8},{16,12},{20,16},{24,20},{28,24},{0,28},{5,1},{9... | collective-permute-start | bytes 49160 | tf_op jit(solution)/shard_map/ppermute | solution.py:26
  13.9 0.8 copy.868
  14.7 0.4 copy_multiply_fusion.1
  15.1 1.1 fusion.68
  16.1 0.7 slice_bitcast_fusion
  17.0 0.4 pad.304
  17.4 0.6 fusion.82
  18.1 0.6 dynamic-slice.122
  18.8 0.8 select_add_fusion.1
  19.5 14.1 %all-gather = f32[4,4,4,2,128]{4,2,3,1,0:T(4,128)S(1)} all-gather(f32[1,4,4,2,128]{4,2,3,1,0:T(4,128)S(1)} %copy.708), channel_id=2, replica_groups=mesh['face'=8,'tile'=4] {'tile'}, dimensions={0}, use_global_device_ids=true | all-gather | bytes 81920 | tf_op jit(solution)/shard_map/all_gather | solution.py:119
  34.8 1.6 scatter.40
  36.4 3.1 %scatter.41 = f32[1,4,2,130,130]{4,3,2,1,0:T(8,128)S(1)} dynamic-update-slice(f32[1,4,2,130,130]{4,3,2,1,0:T(8,128)S(1)} %scatter.40, f32[1,4,2,128,1]{4,3,2,1,0:T(8,128)S(1)} %copy.716, s32[]{:T(128)} %constant.509.clone.1, s32[]{:T(128)} %constant.509.clone.1, s32[]{:T(128)} %constant.509.clone.1, s32[]{:T(128)} %constant.508.clone.1, s32[]{:T(128)} %constant.519.clone.1) | dynamic-update-slice | bytes 8196 | tf_op jit(solution)/shard_map/scatter | solution.py:40
  39.5 2.6 %scatter.44 = f32[1,4,2,130,130]{4,3,2,1,0:T(8,128)S(1)} dynamic-update-slice(f32[1,4,2,130,130]{4,3,2,1,0:T(8,128)S(1)} %scatter.41, f32[1,4,2,1,128]{4,3,2,1,0:T(1,128)S(1)} %bitcast.231, s32[]{:T(128)} %constant.509.clone.1, s32[]{:T(128)} %constant.509.clone.1, s32[]{:T(128)} %constant.509.clone.1, s32[]{:T(128)} %bitcast.20, s32[]{:T(128)} %bitcast.21) | dynamic-update-slice | bytes 8196 | tf_op jit(solution)/shard_map/scatter | solution.py:41
  42.1 1.4 scatter.45
  43.5 0.6 subtract_multiply_fusion.1
  44.5 0.4 copy-done
  45.3 0.8 copy-done.13
  47.0 2.6 %collective-permute-start.3 = (f32[1,1,4,4,2,128]{5,4,3,2,1,0:T(2,128)S(1)}, f32[1,1,4,4,2,128]{5,4,3,2,1,0:T(2,128)S(1)}, u32[]{:S(2)}, u32[]{:S(2)}) collective-permute-start(f32[1,1,4,4,2,128]{5,4,3,2,1,0:T(2,128)S(1)} %fusion.85), channel_id=1, source_target_pairs={{4,0},{8,4},{12,8},{16,12},{20,16},{24,20},{28,24},{0,28},{5,1},{9... | collective-permute-start | bytes 49160 | tf_op jit(solution)/shard_map/ppermute | solution.py:26
  49.6 0.4 pad.305
  50.0 13.4 %all-gather.1 = f32[4,4,4,2,128]{4,2,3,1,0:T(4,128)S(1)} all-gather(f32[1,4,4,2,128]{4,2,3,1,0:T(4,128)S(1)} %copy.722), channel_id=3, replica_groups=mesh['face'=8,'tile'=4] {'tile'}, dimensions={0}, use_global_device_ids=true | all-gather | bytes 81920 | tf_op jit(solution)/shard_map/all_gather | solution.py:119
  64.0 0.6 fusion.80
  64.9 1.0 copy.730
  65.9 1.5 scatter.46
  67.4 4.1 %scatter.49 = f32[1,4,2,130,130]{4,3,2,1,0:T(8,128)S(1)} dynamic-update-slice(f32[1,4,2,130,130]{4,3,2,1,0:T(8,128)S(1)} %scatter.46, f32[1,4,2,128,1]{4,3,2,1,0:T(8,128)} %copy.730, s32[]{:T(128)} %constant.509.clone.1, s32[]{:T(128)} %constant.509.clone.1, s32[]{:T(128)} %constant.509.clone.1, s32[]{:T(128)} %constant.508.clone.1, s32[]{:T(128)} %constant.519.clone.1) | dynamic-update-slice | bytes 8196 | tf_op jit(solution)/shard_map/scatter | solution.py:40
  71.5 2.6 %scatter.50 = f32[1,4,2,130,130]{4,3,2,1,0:T(8,128)S(1)} dynamic-update-slice(f32[1,4,2,130,130]{4,3,2,1,0:T(8,128)S(1)} %scatter.49, f32[1,4,2,1,128]{4,3,2,1,0:T(1,128)S(1)} %bitcast.232, s32[]{:T(128)} %constant.509.clone.1, s32[]{:T(128)} %constant.509.clone.1, s32[]{:T(128)} %constant.509.clone.1, s32[]{:T(128)} %bitcast.20, s32[]{:T(128)} %bitcast.21) | dynamic-update-slice | bytes 8196 | tf_op jit(solution)/shard_map/scatter | solution.py:41
  74.1 1.4 scatter.51
  75.6 0.5 fusion.3
  76.1 0.4 copy-done.5
  76.9 0.7 copy_add_fusion.2
  77.9 0.6 pad_add_fusion.1
  78.5 0.4 add_add_fusion
  78.9 0.5 fusion.8
  79.4 1.1 fusion
  80.6 0.5 copy.755
  81.2 0.7 scatter.54
  82.0 2.0 %scatter.55 = f32[1,4,2,130,130]{4,2,1,3,0:T(2,128)S(1)} dynamic-update-slice(f32[1,4,2,130,130]{4,2,1,3,0:T(2,128)S(1)} %scatter.54, f32[1,4,2,1,128]{4,2,1,3,0:T(2,128)S(1)} %broadcast.864.clone, s32[]{:T(128)} %constant.509.clone.1, s32[]{:T(128)} %constant.509.clone.1, s32[]{:T(128)} %constant.509.clone.1, s32[]{:T(128)} %bitcast.20, s32[]{:T(128)} %bitcast.21) | dynamic-update-slice | bytes 8196 | tf_op jit(solution)/shard_map/transpose(jvp())/scatter | solution.py:41
  83.9 0.7 fusion.66
  84.7 0.4 copy.759
  85.0 0.4 copy.760
  86.0 0.6 copy.761
  86.9 2.9 %collective-permute-start.5 = (f32[1,1,4,4,2,128]{5,4,3,2,1,0:T(2,128)S(1)}, f32[1,1,4,4,2,128]{5,4,3,2,1,0:T(2,128)S(1)}, u32[]{:S(2)}, u32[]{:S(2)}) collective-permute-start(f32[1,1,4,4,2,128]{5,4,3,2,1,0:T(2,128)S(1)} %slice.859), channel_id=1, source_target_pairs={{4,0},{8,4},{12,8},{16,12},{20,16},{24,20},{28,24},{0,28},{5,1},{9... | collective-permute-start | bytes 49160 | tf_op jit(solution)/shard_map/ppermute | solution.py:26
  89.8 31.0 %all-reduce.77.cloned.1.call-done = f32[4,1,4,4,2,128]{5,3,4,2,1,0:T(4,128)} async-done(((f32[4,1,4,4,2,128]{5,3,4,2,1,0:T(4,128)}), f32[4,1,4,4,2,128]{5,3,4,2,1,0:T(4,128)}) %all-reduce.77.cloned.1.call-update) | async-done | bytes 65552
  120.8 1.4 constant_dynamic-slice_fusion.1
  122.2 0.4 copy.763
  122.6 1.0 copy.764
  123.6 2.2 %fusion.2 = f32[1,4,2,128,128]{4,2,1,3,0:T(2,128)S(1)} fusion(f32[1,4,2,130,130]{4,2,1,3,0:T(2,128)S(1)} %scatter.55, f32[1,4,2,128,1]{4,2,1,3,0:T(2,128)} %copy.764, f32[1,4,2,128,1]{4,2,1,3,0:T(2,128)S(1)} %copy.763, f32[1,4,2,1,128]{4,2,1,3,0:T(2,128)S(1)} %get-tuple-element.331, f32[1,4,2,1,128]{4,2,1,3,0:T(2,128)S(1)} %get-tuple-element.328, ...), kind=kLoop, calls=%fused_computation.9 | loop fusion | flops 655360 | bytes 1196032 | tf_op jit(solution)/shard_map/transpose(jvp())/mul | solution.py:85
  126.1 0.7 copy-done.1
  127.0 0.3 fusion.45
  127.3 0.4 copy-done.18
  127.8 0.7 fusion.9
  128.7 1.2 pad_add_fusion
  130.0 1.4 scatter.56
  131.5 2.6 %scatter.59 = f32[1,4,2,130,130]{4,3,2,1,0:T(8,128)S(1)} dynamic-update-slice(f32[1,4,2,130,130]{4,3,2,1,0:T(8,128)S(1)} %scatter.56, f32[1,4,2,1,128]{4,3,2,1,0:T(1,128)S(1)} %broadcast.864.clone.1, s32[]{:T(128)} %constant.509.clone.1, s32[]{:T(128)} %constant.509.clone.1, s32[]{:T(128)} %constant.509.clone.1, s32[]{:T(128)} %bitcast.20, s32[]{:T(128)} %bitcast.21) | dynamic-update-slice | bytes 8196 | tf_op jit(solution)/shard_map/transpose(jvp())/scatter | solution.py:41
  134.2 0.5 slice_reduce_fusion.1
  135.0 0.2 fusion.59
  135.5 0.6 copy.775
  136.3 2.7 %collective-permute-start.7 = (f32[1,1,4,4,2,128]{5,4,3,2,1,0:T(2,128)S(1)}, f32[1,1,4,4,2,128]{5,4,3,2,1,0:T(2,128)S(1)}, u32[]{:S(2)}, u32[]{:S(2)}) collective-permute-start(f32[1,1,4,4,2,128]{5,4,3,2,1,0:T(2,128)S(1)} %slice.865), channel_id=1, source_target_pairs={{4,0},{8,4},{12,8},{16,12},{20,16},{24,20},{28,24},{0,28},{5,1},{9... | collective-permute-start | bytes 49160 | tf_op jit(solution)/shard_map/ppermute | solution.py:26
  139.1 0.8 copy.780
  140.0 30.1 %all-reduce.79.cloned.1.call-done = f32[4,1,4,4,2,128]{5,3,4,2,1,0:T(4,128)} async-done(((f32[4,1,4,4,2,128]{5,3,4,2,1,0:T(4,128)}), f32[4,1,4,4,2,128]{5,3,4,2,1,0:T(4,128)}) %all-reduce.79.cloned.1.call-update) | async-done | bytes 65552
  170.1 1.4 constant_dynamic-slice_fusion
  171.9 1.1 fusion.1
  (156 shorter events, 8.1 us)
Async XLA Ops:
  7.2 113.6 %all-reduce.77.cloned.1.call-start = ((), (), s32[]{:S(2)}) async-start(), calls=%async_computation | async-start | bytes 131072
  10.0 4.7 %copy-start.10 = (f32[1,4,2,128,128]{4,3,2,1,0:T(8,128)S(1)}, f32[1,4,2,128,128]{4,3,2,1,0:T(8,128)}, u32[]{:S(2)}) copy-start(f32[1,4,2,128,128]{4,3,2,1,0:T(8,128)} %param.43) | copy-start | bytes 1572868
  10.4 23.2 %collective-permute-start = (f32[1,1,4,4,2,128]{5,4,3,2,1,0:T(2,128)S(1)}, f32[1,1,4,4,2,128]{5,4,3,2,1,0:T(2,128)S(1)}, u32[]{:S(2)}, u32[]{:S(2)}) collective-permute-start(f32[1,1,4,4,2,128]{5,4,3,2,1,0:T(2,128)S(1)} %fusion.86), channel_id=1, source_target_pairs={{0,4},{4,8},{8,12},{12,16},{16,20},{20,24},{24,28},{28,0},{1,5},{5... | collective-permute-start | bytes 49160 | tf_op jit(solution)/shard_map/ppermute | solution.py:23
  11.0 22.7 %collective-permute-start.1 = (f32[1,1,4,4,2,128]{5,4,3,2,1,0:T(2,128)S(1)}, f32[1,1,4,4,2,128]{5,4,3,2,1,0:T(2,128)S(1)}, u32[]{:S(2)}, u32[]{:S(2)}) collective-permute-start(f32[1,1,4,4,2,128]{5,4,3,2,1,0:T(2,128)S(1)} %fusion.86), channel_id=1, source_target_pairs={{4,0},{8,4},{12,8},{16,12},{20,16},{24,20},{28,24},{0,28},{5,1},{9... | collective-permute-start | bytes 49160 | tf_op jit(solution)/shard_map/ppermute | solution.py:26
  14.7 2.2 %copy-start.19 = (s32[1,4]{1,0:T(1,128)S(1)}, s32[1,4]{1,0:T(1,128)}, u32[]{:S(2)}) copy-start(s32[1,4]{1,0:T(1,128)} %param.44) | copy-start | bytes 52
  14.7 2.2 %copy-start.20 = (s32[1,4]{1,0:T(1,128)S(1)}, s32[1,4]{1,0:T(1,128)}, u32[]{:S(2)}) copy-start(s32[1,4]{1,0:T(1,128)} %param.45) | copy-start | bytes 52
  16.1 2.6 %copy-start.4 = (f32[1,1,2,128,128]{4,1,3,2,0:T(1,128)}, f32[1,1,2,128,128]{4,1,3,2,0:T(1,128)S(1)}, u32[]{:S(2)}) copy-start(f32[1,1,2,128,128]{4,1,3,2,0:T(1,128)S(1)} %get-tuple-element.265) | copy-start | bytes 393220
  17.0 1.2 copy-start.21
  17.0 1.8 copy-start.17
  18.1 45.6 %copy-start.15 = (pred[1,4,1,1,1,1,24]{6,1,5,4,3,2,0:T(4,128)(4,1)}, pred[1,4,1,1,1,1,24]{6,1,5,4,3,2,0:T(4,128)(4,1)S(1)}, u32[]{:S(2)}) copy-start(pred[1,4,1,1,1,1,24]{6,1,5,4,3,2,0:T(4,128)(4,1)S(1)} %fusion.56) | copy-start | bytes 292
  44.1 0.8 copy-start
  44.1 1.0 copy-start.2
  45.1 1.0 copy-start.13
  46.9 16.4 %collective-permute-start.2 = (f32[1,1,4,4,2,128]{5,4,3,2,1,0:T(2,128)S(1)}, f32[1,1,4,4,2,128]{5,4,3,2,1,0:T(2,128)S(1)}, u32[]{:S(2)}, u32[]{:S(2)}) collective-permute-start(f32[1,1,4,4,2,128]{5,4,3,2,1,0:T(2,128)S(1)} %fusion.85), channel_id=1, source_target_pairs={{0,4},{4,8},{8,12},{12,16},{16,20},{20,24},{24,28},{28,0},{1,5},{5... | collective-permute-start | bytes 49160 | tf_op jit(solution)/shard_map/ppermute | solution.py:23
  47.0 16.4 %collective-permute-start.3 = (f32[1,1,4,4,2,128]{5,4,3,2,1,0:T(2,128)S(1)}, f32[1,1,4,4,2,128]{5,4,3,2,1,0:T(2,128)S(1)}, u32[]{:S(2)}, u32[]{:S(2)}) collective-permute-start(f32[1,1,4,4,2,128]{5,4,3,2,1,0:T(2,128)S(1)} %fusion.85), channel_id=1, source_target_pairs={{4,0},{8,4},{12,8},{16,12},{20,16},{24,20},{28,24},{0,28},{5,1},{9... | collective-permute-start | bytes 49160 | tf_op jit(solution)/shard_map/ppermute | solution.py:26
  65.9 5.6 %copy-start.14 = (f32[1,1,4,2,128]{4,3,2,1,0:T(2,128)S(1)}, f32[1,1,4,2,128]{4,3,2,1,0:T(2,128)}, u32[]{:S(2)}) copy-start(f32[1,1,4,2,128]{4,3,2,1,0:T(2,128)} %get-tuple-element.333) | copy-start | bytes 12292
  75.6 0.9 copy-start.5
  75.6 1.0 copy-start.7
  75.6 1.0 copy-start.8
  77.9 1.0 copy-start.11
  77.9 1.0 copy-start.12
  84.6 1.0 copy-start.16
  85.4 38.2 %copy-start.9 = (f32[2,128,128]{2,0,1:T(2,128)S(1)}, f32[2,128,128]{2,0,1:T(2,128)}, u32[]{:S(2)}) copy-start(f32[2,128,128]{2,0,1:T(2,128)} %copy.868) | copy-start | bytes 393220
  86.7 83.4 %all-reduce.79.cloned.1.call-start = ((), (), s32[]{:S(2)}) async-start(), calls=%async_computation.1 | async-start | bytes 131072
  86.8 35.4 %collective-permute-start.4 = (f32[1,1,4,4,2,128]{5,4,3,2,1,0:T(2,128)S(1)}, f32[1,1,4,4,2,128]{5,4,3,2,1,0:T(2,128)S(1)}, u32[]{:S(2)}, u32[]{:S(2)}) collective-permute-start(f32[1,1,4,4,2,128]{5,4,3,2,1,0:T(2,128)S(1)} %slice.857), channel_id=1, source_target_pairs={{0,4},{4,8},{8,12},{12,16},{16,20},{20,24},{24,28},{28,0},{1,5},{5... | collective-permute-start | bytes 49160 | tf_op jit(solution)/shard_map/ppermute | solution.py:23
  86.9 35.3 %collective-permute-start.5 = (f32[1,1,4,4,2,128]{5,4,3,2,1,0:T(2,128)S(1)}, f32[1,1,4,4,2,128]{5,4,3,2,1,0:T(2,128)S(1)}, u32[]{:S(2)}, u32[]{:S(2)}) collective-permute-start(f32[1,1,4,4,2,128]{5,4,3,2,1,0:T(2,128)S(1)} %slice.859), channel_id=1, source_target_pairs={{4,0},{8,4},{12,8},{16,12},{20,16},{24,20},{28,24},{0,28},{5,1},{9... | collective-permute-start | bytes 49160 | tf_op jit(solution)/shard_map/ppermute | solution.py:26
  125.8 1.0 copy-start.1
  125.8 1.2 copy-start.3
  127.0 0.7 copy-start.18
  134.2 4.8 %copy-start.6 = (f32[1,1,4,128,128]{4,2,3,1,0:T(4,128)S(1)}, f32[1,1,4,128,128]{4,2,3,1,0:T(4,128)}, u32[]{:S(2)}) copy-start(f32[1,1,4,128,128]{4,2,3,1,0:T(4,128)} %slice_bitcast_fusion) | copy-start | bytes 786436
  136.2 35.2 %collective-permute-start.6 = (f32[1,1,4,4,2,128]{5,4,3,2,1,0:T(2,128)S(1)}, f32[1,1,4,4,2,128]{5,4,3,2,1,0:T(2,128)S(1)}, u32[]{:S(2)}, u32[]{:S(2)}) collective-permute-start(f32[1,1,4,4,2,128]{5,4,3,2,1,0:T(2,128)S(1)} %slice.863), channel_id=1, source_target_pairs={{0,4},{4,8},{8,12},{12,16},{16,20},{20,24},{24,28},{28,0},{1,5},{5... | collective-permute-start | bytes 49160 | tf_op jit(solution)/shard_map/ppermute | solution.py:23
  136.3 35.1 %collective-permute-start.7 = (f32[1,1,4,4,2,128]{5,4,3,2,1,0:T(2,128)S(1)}, f32[1,1,4,4,2,128]{5,4,3,2,1,0:T(2,128)S(1)}, u32[]{:S(2)}, u32[]{:S(2)}) collective-permute-start(f32[1,1,4,4,2,128]{5,4,3,2,1,0:T(2,128)S(1)} %slice.865), channel_id=1, source_target_pairs={{4,0},{8,4},{12,8},{16,12},{20,16},{24,20},{28,24},{0,28},{5,1},{9... | collective-permute-start | bytes 49160 | tf_op jit(solution)/shard_map/ppermute | solution.py:26
Sparse Core Ops, SparseCore 0:
  86.8 33.9 all-reduce.76
  136.3 33.6 all-reduce.78
where the time goes:
time: 181 us; the launch traced here: 180 us
  waiting for transfers between devices  61.2 us (34%)
  local copies, waits for them, and re-layouts  47.5 us (26%)
  blocking collectives  27.5 us (15%)
  between operations  15.6 us (9%)
  other arithmetic  15.3 us (8%)
  starting transfers between devices  11.9 us (7%)
    unnamed x4, waiting for transfers between devices  61.2 us
    all_gather x2, blocking collectives, gather_rims(): grouped = lax.all_gather(strips, 'tile', axis=0, tiled=True)  27.5 us
    ppermute x4, starting transfers between devices, with_halo(): lax.ppermute(lax.slice_in_dim(block, 0, width, axis=dim), axis, backward)  11.2 us
    scatter x4, local copies, waits for them, and re-layouts, place_halo(): padded = padded.at[..., 0, 1:-1].set(halos[:, 2])  9.83 us
    unnamed x55, local copies, waits for them, and re-layouts  8.99 us
    scatter x2, local copies, waits for them, and re-layouts, place_halo(): padded = padded.at[..., 1:-1, -1].set(halos[:, 1])  7.21 us
    scatter x4, local copies, waits for them, and re-layouts, place_halo(): padded = padded.at[..., -1, 1:-1].set(halos[:, 3])  4.87 us
  transfers between devices with their start and end apart: 10, of which 2 were waited for; matrix products, arithmetic and copies ran while one was open for 5% of the time, Pallas kernels for 0%

commit v1 on v0

v1 whole, which is shorter than its diff:
```python
import jax
import jax.numpy as jnp
from jax import lax
from jax.experimental import pallas as pl
from jax.experimental.pallas import tpu as pltpu
from jax.sharding import PartitionSpec as P

MESH = pl.DeviceIdType.MESH
WEST, EAST, SOUTH, NORTH = 0, 1, 2, 3
SIGN = (-1.0, 1.0, -1.0, 1.0)
TOP = 8
ROWS = 16
F32 = jnp.float32


def iota(shape, axis):
    return lax.broadcasted_iota(jnp.int32, shape, axis)


def up(x, n):
    return pltpu.roll(x, (-n) % 8, 0)


def lift(x, side):
    row = iota((8, 128), 0)
    near, far = (2, 4) if side < 2 else (4, 6)
    return jnp.where(row < 2, up(x, far), jnp.where(row < 4, up(x, near), 0.0))


def lower(theta, salt, side):
    row = iota((8, 128), 0)
    first = 4 if side < 2 else 6
    here = (row >= first) & (row < first + 2)
    return jnp.where(here, up(theta, -first) + up(salt, 2 - first), 0.0)


def rim_gradient(m, x, side):
    row = iota((8, 128), 0)
    weight = jnp.where(row < 2, 0.125, -0.1)
    return m * (0.15 - 0.5 * SIGN[side] * lift(x, side)) + SIGN[side] * weight * lift(m, side)


def rim_step(halo, x, side):
    pressure = lower(0.125 * halo, -0.1 * halo, side)
    return halo * (0.15 - 0.5 * SIGN[side] * lift(x, side)) + SIGN[side] * pressure


def rim_velocity(m, halo, side):
    product = m * halo
    return -0.5 * SIGN[side] * lower(product, product, side)


def crossed(c):
    lane = iota((8, 128), 1)
    first, last = lane == 0, lane == 127

    def at(low, high):
        return jnp.where(first, low, jnp.where(last, high, 0.0))

    right = [pltpu.roll(v, 1, 1) for v in c]
    left = [pltpu.roll(v, 127, 1) for v in c]
    return [
        c[WEST] + at(c[SOUTH], left[NORTH]),
        c[EAST] + at(right[SOUTH], c[NORTH]),
        c[SOUTH] + at(c[WEST], left[EAST]),
        c[NORTH] + at(right[WEST], c[EAST]),
    ]


def from_west(x):
    return jnp.where(iota(x.shape, 1) == 0, 0.0, pltpu.roll(x, 1, 1))


def from_east(x):
    return jnp.where(iota(x.shape, 1) == 127, 0.0, pltpu.roll(x, 127, 1))


def pick_columns(planes):
    lane = iota(planes[0].shape, 1)
    out = jnp.zeros_like(planes[0])
    for p, x in enumerate(planes):
        out = jnp.where(lane == p, pltpu.roll(x, p, 1) if p else x, out)
        out = jnp.where(lane == 8 + p, pltpu.roll(x, 9 + p, 1), out)
    return out


def put_columns(columns, p):
    lane = iota(columns.shape, 1)
    west = pltpu.roll(columns, 128 - p, 1) if p else columns
    east = pltpu.roll(columns, 119 - p, 1)
    return jnp.where(lane == 0, west, jnp.where(lane == 127, east, 0.0))


def step_block(xp, drive, mask, r):
    def at(p, shift=0):
        return xp[p, TOP + r + shift : TOP + r + shift + ROWS, :]

    out = [None] * 8
    for l in range(2):
        c = [at(2 * f + l) for f in range(4)]
        other = [at(2 * f + 1 - l) for f in range(2)]
        new = []
        grads = []
        for f in range(4):
            e, w = from_east(c[f]), from_west(c[f])
            n, s = at(2 * f + l, 1), at(2 * f + l, -1)
            lap = e + w + n + s - 4.0 * c[f]
            grads.append((0.5 * (e - w), 0.5 * (n - s)))
            new.append(c[f] + 0.15 * lap)
        u, v = c[2], c[3]
        for f in range(2):
            new[f] = new[f] - (u * grads[f][0] + v * grads[f][1]) + 0.1 * (other[f] - c[f])
        new[2] = new[2] + 0.3 * v - 0.25 * (0.8 * grads[1][0] - grads[0][0]) - 0.05 * u
        new[3] = new[3] - 0.3 * u - 0.25 * (0.8 * grads[1][1] - grads[0][1]) - 0.05 * v
        for f in range(4):
            if l == 0:
                new[f] = new[f] + drive[f, r : r + ROWS, :]
            out[2 * f + l] = new[f] * mask[l, r : r + ROWS, :]
    return out


def back_block(xp, mp, r):
    def x_at(p, shift=0):
        return xp[p, TOP + r + shift : TOP + r + shift + ROWS, :]

    def m_at(p, shift=0):
        return mp[p, TOP + r + shift : TOP + r + shift + ROWS, :]

    out = [None] * 8
    for l in range(2):
        u = 0.5 * x_at(4 + l)
        v_s, v_n = 0.5 * x_at(6 + l, -1), 0.5 * x_at(6 + l, 1)
        c, d = m_at(4 + l), m_at(6 + l)
        c_s, c_n, d_s, d_n = m_at(4 + l, -1), m_at(4 + l, 1), m_at(6 + l, -1), m_at(6 + l, 1)
        g_u = 0.15 * (from_west(c) + from_east(c) + c_s + c_n) + 0.35 * c - 0.3 * d
        g_v = 0.15 * (from_west(d) + from_east(d) + d_s + d_n) + 0.35 * d + 0.3 * c
        for f, k in ((0, 0.125), (1, -0.1)):
            p = 2 * f + l
            a, a_s, a_n, a_o = m_at(p), m_at(p, -1), m_at(p, 1), m_at(2 * f + 1 - l)
            kc = k * c
            au = a * u
            a15 = 0.15 * a
            g = from_west(a15 - au + kc) + from_east(a15 + au - kc)
            g = g + a_s * (0.15 - v_s) + a_n * (0.15 + v_n) + k * (d_s - d_n)
            out[p] = g + 0.3 * a + 0.1 * a_o
            x = x_at(p)
            half = 0.5 * a
            g_u = g_u - half * (from_east(x) - from_west(x))
            g_v = g_v - half * (x_at(p, 1) - x_at(p, -1))
        out[4 + l], out[6 + l] = g_u, g_v
    return out


def kernel(
    nb, rot, wet, state, forcing, cot, levels, sg_out, fg_out,
    st, drive, ctv, lev, mask, x0p, x1p, m2p, m1p, part, sgv, fgv, cols,
    a_send, a_recv, t_send, t_recv,
    bg_send, bl_send, bu_send, bg_recv, bf_recv,
    dg_send, dl_send, du_send, dg_recv, df_recv,
    in_sem, out_sem, send_sem, recv_sem,
):
    group, faces = lax.axis_size("tile"), lax.axis_size("face")
    face, tile = lax.axis_index("face"), lax.axis_index("tile")
    below, above = lax.rem(face + faces - 1, faces), lax.rem(face + 1, faces)
    peers = [lax.rem(tile + j, group) for j in range(1, group)]
    me = face * group + tile
    blocks = range(0, 128, ROWS)

    loads = [
        pltpu.make_async_copy(state.at[0], st, in_sem.at[0]),
        pltpu.make_async_copy(levels.at[0], lev, in_sem.at[1]),
        pltpu.make_async_copy(cot.at[0], ctv, in_sem.at[2]),
        pltpu.make_async_copy(forcing.at[0, 0], drive, in_sem.at[3]),
    ]
    for load in loads:
        load.start()
    barrier = pltpu.get_barrier_semaphore()
    for peer in peers:
        pl.semaphore_signal(barrier, inc=1, device_id=(face, peer), device_id_type=MESH)
    for other in (below, above):
        pl.semaphore_signal(barrier, inc=1, device_id=(other, tile), device_id_type=MESH)

    pad = jnp.zeros((8, TOP, 128), F32)
    for ref in (x0p, x1p, m2p, m1p):
        ref[:, 0:TOP, :] = pad
        ref[:, TOP + 128 : 2 * TOP + 128, :] = pad

    side_of = [lax.rem(rot[0, k], 4) for k in range(4)]
    flip = [rot[0, k] >= 4 for k in range(4)]
    source = [nb[0, k] for k in range(4)]
    valid = [s >= 0 for s in source]
    source_tile = [lax.rem(jnp.maximum(s, 0), group) for s in source]
    code = [jnp.where(valid[k], source[k] * 4 + side_of[k], -1) for k in range(4)]
    is_wet = wet[0] == 1
    lane = iota((8, 128), 1)
    row = iota((8, 128), 0)

    def turn(x, k):
        back = jnp.take_along_axis(x, 127 - lane, axis=1)
        return jnp.where(flip[k], back, x)

    table = jnp.full((8, 128), -1, jnp.int32)
    for k in range(4):
        table = jnp.where(row == k, code[k], table)
    t_send[...] = table
    t_recv[tile] = table

    def send(phase, to_peer, to_below, to_above):
        copies = []
        for j, peer in reversed(list(enumerate(peers))):
            src, dst = to_peer
            copies.append(
                pltpu.make_async_remote_copy(
                    src, dst, send_sem.at[phase, j], recv_sem.at[phase, tile],
                    device_id=(face, peer), device_id_type=MESH,
                )
            )
        for j, (src, dst), other, slot in (
            (group - 1, to_below, below, group + 1),
            (group, to_above, above, group),
        ):
            copies.append(
                pltpu.make_async_remote_copy(
                    src, dst, send_sem.at[phase, j], recv_sem.at[phase, slot],
                    device_id=(other, tile), device_id_type=MESH,
                )
            )
        for copy in copies:
            copy.start()
        return copies

    def receive(phase, from_peer, from_below, from_above):
        for j, peer in enumerate(peers):
            ref = from_peer(peer)
            pltpu.make_async_remote_copy(
                ref, ref, send_sem.at[phase, j], recv_sem.at[phase, peer],
                device_id=(face, peer), device_id_type=MESH,
            ).wait_recv()
        for ref, slot, other in ((from_below, group, below), (from_above, group + 1, above)):
            pltpu.make_async_remote_copy(
                ref, ref, send_sem.at[phase, group], recv_sem.at[phase, slot],
                device_id=(other, tile), device_id_type=MESH,
            ).wait_recv()

    loads[1].wait()
    loads[0].wait()
    for r in blocks:
        deep = jnp.where(is_wet, lev[r : r + ROWS, :], 0)
        masks = [(deep > l).astype(F32) for l in range(2)]
        planes = []
        for l in range(2):
            mask[l, r : r + ROWS, :] = masks[l]
        for p in range(8):
            x = st[p // 2, p % 2, r : r + ROWS, :] * masks[p % 2]
            x0p[p, TOP + r : TOP + r + ROWS, :] = x
            planes.append(x)
        picked = pick_columns(planes)
        wide = iota(picked.shape, 1)
        for l in range(2):
            picked = jnp.where(wide == 16 + l, pltpu.roll(masks[l], 16 + l, 1), picked)
            picked = jnp.where(wide == 18 + l, pltpu.roll(masks[l], 19 + l, 1), picked)
        cols[0, r : r + ROWS, :] = picked

    def even_odd(even, odd):
        return jnp.where(
            lax.rem(row, 2) == 0, jnp.broadcast_to(even, (8, 128)), jnp.broadcast_to(odd, (8, 128))
        )

    def rows_of(ref, at):
        return jnp.concatenate([ref[p, at : at + 1, :] for p in range(8)], axis=0)

    turned = jnp.transpose(cols[0])
    x0 = [turned[0:8], turned[8:16], rows_of(x0p, TOP), rows_of(x0p, TOP + 127)]
    rim_mask = [
        even_odd(turned[16:17], turned[17:18]),
        even_odd(turned[18:19], turned[19:20]),
        even_odd(mask[0, 0:1, :], mask[1, 0:1, :]),
        even_odd(mask[0, 127:128, :], mask[1, 127:128, :]),
    ]
    for k in range(4):
        a_send[k] = x0[k]
        a_recv[tile, k] = x0[k]
    pl.semaphore_wait(barrier, group + 1)
    copies = send(
        0, (a_send, a_recv.at[tile]), (a_send, a_recv.at[group + 1]), (a_send, a_recv.at[group])
    )
    copies += send(
        1, (t_send, t_recv.at[tile]), (t_send, t_recv.at[group + 1]), (t_send, t_recv.at[group])
    )

    loads[2].wait()
    for r in blocks:
        planes = []
        for p in range(8):
            m = ctv[p // 2, p % 2, r : r + ROWS, :] * mask[p % 2, r : r + ROWS, :]
            m2p[p, TOP + r : TOP + r + ROWS, :] = m
            if p % 2 == 0:
                fgv[1, p // 2, r : r + ROWS, :] = m
            planes.append(m)
        cols[1, r : r + ROWS, :] = pick_columns(planes)
    fg_second = pltpu.make_async_copy(fgv.at[1], fg_out.at[0, 1], out_sem.at[0])
    fg_second.start()
    loads[3].wait()
    for r in blocks:
        planes = step_block(x0p, drive, mask, r)
        for p in range(8):
            x1p[p, TOP + r : TOP + r + ROWS, :] = planes[p]
        cols[2, r : r + ROWS, :] = pick_columns(planes)
    turned = jnp.transpose(cols[1])
    m2 = [turned[0:8], turned[8:16], rows_of(m2p, TOP), rows_of(m2p, TOP + 127)]
    turned = jnp.transpose(cols[2])
    x1 = [turned[0:8], turned[8:16], rows_of(x1p, TOP), rows_of(x1p, TOP + 127)]

    receive(0, lambda t: a_recv.at[t], a_recv.at[group], a_recv.at[group + 1])
    place = [group, group + 1, source_tile[SOUTH], source_tile[NORTH]]

    def usable(x, k):
        return x if k < 2 else jnp.where(valid[k], x, 0.0)

    halo0 = [usable(turn(a_recv[place[k], side_of[k]], k), k) for k in range(4)]
    fix1 = [rim_mask[k] * rim_step(halo0[k], x0[k], k) for k in range(4)]
    more = crossed(fix1)
    x1 = [x1[k] + more[k] for k in range(4)]
    back2 = [turn(rim_gradient(m2[k], x1[k], k), k) for k in range(4)]
    pairs = [
        jnp.where(row < 4, x1[WEST], up(x1[EAST], 4)),
        jnp.where(row < 4, x1[SOUTH], up(x1[NORTH], 4)),
    ]
    for i, value in enumerate(pairs + [back2[SOUTH], back2[NORTH]]):
        bg_send[i] = value
        bg_recv[tile, i] = value
    for i, value in enumerate(pairs + [back2[WEST]]):
        bl_send[i] = value
    for i, value in enumerate(pairs + [back2[EAST]]):
        bu_send[i] = value
    copies += send(2, (bg_send, bg_recv.at[tile]), (bl_send, bf_recv.at[1]), (bu_send, bf_recv.at[0]))

    def put_rims(fix, index, add):
        tall = jnp.concatenate([fix[WEST], fix[EAST], jnp.zeros((112, 128), F32)], axis=0)
        cols[index] = jnp.transpose(tall)
        for p in range(8):
            add(p, 0, 1, fix[SOUTH][p : p + 1])
            add(p, 127, 1, fix[NORTH][p : p + 1])

    def add_x1(p, r, n, value):
        x1p[p, TOP + r : TOP + r + n, :] = x1p[p, TOP + r : TOP + r + n, :] + value

    put_rims(fix1, 3, add_x1)
    for r in blocks:
        columns = cols[3, r : r + ROWS, :]
        for p in range(8):
            add_x1(p, r, ROWS, put_columns(columns, p))
    for r in blocks:
        planes = back_block(x1p, m2p, r)
        for p in range(8):
            part[p, r : r + ROWS, :] = planes[p]
        cols[4, r : r + ROWS, :] = pick_columns(planes)
    turned = jnp.transpose(cols[4])
    g1 = [turned[0:8], turned[8:16], rows_of(part, 0), rows_of(part, 127)]

    receive(1, lambda t: t_recv.at[t], t_recv.at[group], t_recv.at[group + 1])
    receive(2, lambda t: bg_recv.at[t], bf_recv.at[0], bf_recv.at[1])

    def pair(ref, at, k):
        both = ref[at, lax.div(side_of[k], 2)]
        return jnp.where(lax.rem(side_of[k], 2) == 1, up(both, 4), both)

    halo1 = [
        pair(bf_recv, 0, WEST), pair(bf_recv, 1, EAST),
        pair(bg_recv, source_tile[SOUTH], SOUTH), pair(bg_recv, source_tile[NORTH], NORTH),
    ]
    halo1 = [usable(turn(halo1[k], k), k) for k in range(4)]

    senders = [(t, k) for t in range(group) for k in (SOUTH, NORTH)] + [(group, EAST), (group + 1, WEST)]
    codes = [jnp.broadcast_to(t_recv[t, k : k + 1, :], (8, 128)) for t, k in senders]

    def returned(values, k):
        total = jnp.zeros((8, 128), F32)
        for seen, value in zip(codes, values):
            total = total + jnp.where(seen == me * 4 + k, value, 0.0)
        return total

    values = [bg_recv[t, k] for t in range(group) for k in (2, 3)] + [bf_recv[0, 2], bf_recv[1, 2]]
    fix2 = [rim_velocity(m2[k], halo1[k], k) + returned(values, k) for k in range(4)]
    more = crossed(fix2)
    m1 = [rim_mask[k] * (g1[k] + more[k]) for k in range(4)]
    back1 = [turn(rim_gradient(m1[k], x0[k], k), k) for k in range(4)]
    for i, k in enumerate((SOUTH, NORTH)):
        dg_send[i] = back1[k]
        dg_recv[tile, i] = back1[k]
    dl_send[0] = back1[WEST]
    du_send[0] = back1[EAST]
    copies += send(3, (dg_send, dg_recv.at[tile]), (dl_send, df_recv.at[1]), (du_send, df_recv.at[0]))

    def add_part(p, r, n, value):
        part[p, r : r + n, :] = part[p, r : r + n, :] + value

    put_rims(fix2, 5, add_part)
    for r in blocks:
        columns = cols[5, r : r + ROWS, :]
        for p in range(8):
            m = part[p, r : r + ROWS, :] + put_columns(columns, p)
            m = m * mask[p % 2, r : r + ROWS, :]
            m1p[p, TOP + r : TOP + r + ROWS, :] = m
            if p % 2 == 0:
                fgv[0, p // 2, r : r + ROWS, :] = m
    fg_first = pltpu.make_async_copy(fgv.at[0], fg_out.at[0, 0], out_sem.at[1])
    fg_first.start()
    for r in blocks:
        planes = back_block(x0p, m1p, r)
        for p in range(8):
            part[p, r : r + ROWS, :] = planes[p] * mask[p % 2, r : r + ROWS, :]
    own = [rim_velocity(m1[k], halo0[k], k) for k in range(4)]

    receive(3, lambda t: dg_recv.at[t], df_recv.at[0], df_recv.at[1])
    values = [dg_recv[t, i] for t in range(group) for i in (0, 1)] + [df_recv[0, 0], df_recv[1, 0]]
    fix3 = [rim_mask[k] * (own[k] + returned(values, k)) for k in range(4)]
    put_rims(fix3, 6, add_part)
    for r in blocks:
        columns = cols[6, r : r + ROWS, :]
        for p in range(8):
            sgv[p // 2, p % 2, r : r + ROWS, :] = part[p, r : r + ROWS, :] + put_columns(columns, p)
    sg_copy = pltpu.make_async_copy(sgv, sg_out.at[0], out_sem.at[2])
    sg_copy.start()
    for copy in copies:
        copy.wait_send()
    fg_second.wait()
    fg_first.wait()
    sg_copy.wait()


def shards(state, forcing, cotangent, neighbour, rotation, wet, levels):
    group = lax.axis_size("tile")
    anywhere = pl.BlockSpec(memory_space=pl.ANY)
    scalars = pl.BlockSpec(memory_space=pltpu.SMEM)
    fields, depth, side = state.shape[1], state.shape[2], state.shape[3]
    vm = lambda *shape: pltpu.VMEM(shape, F32)
    whole = lambda *shape: pltpu.VMEM(shape, jnp.int32)
    padded = vm(8, side + 2 * TOP, side)
    return pl.pallas_call(
        kernel,
        out_shape=(
            jax.ShapeDtypeStruct(state.shape, F32),
            jax.ShapeDtypeStruct(forcing.shape, F32),
        ),
        in_specs=[scalars] * 3 + [anywhere] * 4,
        out_specs=(anywhere, anywhere),
        scratch_shapes=[
            vm(fields, depth, side, side), vm(fields, side, side), vm(fields, depth, side, side),
            whole(side, side), vm(depth, side, side),
            padded, padded, padded, padded,
            vm(8, side, side), vm(fields, depth, side, side), vm(2, fields, side, side),
            vm(7, side, side),
            vm(4, 8, side), vm(group + 2, 4, 8, side),
            whole(8, side), whole(group + 2, 8, side),
            vm(4, 8, side), vm(3, 8, side), vm(3, 8, side), vm(group, 4, 8, side), vm(2, 3, 8, side),
            vm(2, 8, side), vm(1, 8, side), vm(1, 8, side), vm(group, 2, 8, side), vm(2, 1, 8, side),
            pltpu.SemaphoreType.DMA((4,)), pltpu.SemaphoreType.DMA((3,)),
            pltpu.SemaphoreType.DMA((4, group + 1)), pltpu.SemaphoreType.DMA((4, group + 2)),
        ],
        compiler_params=pltpu.CompilerParams(
            collective_id=0, has_side_effects=True, vmem_limit_bytes=32 * 1024 * 1024
        ),
        name="window",
    )(neighbour, rotation, wet, state, forcing, cotangent, levels)


def solution(mesh):
    placed = (
        P(("face", "tile"), None, None, None, None),
        P(("face", "tile"), None, None, None, None),
        P(("face", "tile"), None, None, None, None),
        P(("face", "tile"), None),
        P(("face", "tile"), None),
        P(("face", "tile")),
        P(("face", "tile"), None, None),
    )
    return jax.shard_map(
        shards,
        mesh=mesh,
        in_specs=placed,
        out_specs=(
            P(("face", "tile"), None, None, None, None),
            P(("face", "tile"), None, None, None, None),
        ),
        check_vma=False,
    )
```

time: 181 us -> 25.8 us (0.14)
  waiting for transfers between devices: 61.2 us -> 0 us
  local copies, waits for them, and re-layouts: 47.5 us -> 5.55 us
  blocking collectives: 27.5 us -> 0 us
  Pallas kernels: 0 us -> 18.5 us
  other arithmetic: 15.3 us -> 0 us
  between operations: 15.6 us -> 1.35 us
  starting transfers between devices: 11.9 us -> 0 us
    unnamed x4 -> x0, waiting for transfers between devices: 61.2 us -> none
    all_gather x2 -> x0, blocking collectives: 27.5 us -> none  [gather_rims(): grouped = lax.all_gather(strips, 'tile', axis=0, tiled=True)]
    scatter x12 -> x0, local copies, waits for them, and re-layouts: 25 us -> none  [the longest x4 9.83 us: place_halo(): padded = padded.at[..., 0, 1:-1].set(halos[:, 2])]
    pallas_call x0 -> x1, Pallas kernels: none -> 18.5 us  [shards(): pl.pallas_call(kernel, out_shape=(jax.ShapeDtypeStruct(state.shape, F32),...]
    ppermute x8 -> x0, starting transfers between devices: 11.8 us -> none  [the longest x4 11.2 us: with_halo(): lax.ppermute(lax.slice_in_dim(block, 0, width, axis=dim), axis, backward)]
    add_any x15 -> x0, other arithmetic: 6.71 us -> none  [the longest x2 2.36 us: step_tiles(): centre = padded[..., 1:-1, 1:-1]]
    mul x14 -> x0, other arithmetic: 6.56 us -> none  [the longest x3 2.61 us: step_tiles(): return result * mask[:, None]]
    another operation x20 -> x0, local copies, waits for them, and re-layouts: 5.65 us -> none
  transfers between devices with their start and end apart: 10 -> 0, of which waited for: 2 -> 0; matrix products, arithmetic and copies ran while one was open for 5% -> 0% of each run, Pallas kernels for 0% -> 0%
where the time goes in v1:
time: 25.8 us; the launch traced here: 25.4 us
  Pallas kernels  18.5 us (72%)
  local copies, waits for them, and re-layouts  5.55 us (22%)
  between operations  1.35 us (5%)
    pallas_call x1, Pallas kernels, shards(): pl.pallas_call(kernel, out_shape=(jax.ShapeDtypeStruct(state.shape, F32),...  18.5 us
    unnamed x14, local copies, waits for them, and re-layouts  5.55 us

profile of v1, /device:TPU:0, one launch (start us, length us, event | category | flops | bytes accessed | tf_op | source)
XLA Modules:
  0.0 25.4 jit_solution(7684851855343163686)
XLA Ops:
  0.6 0.0 copy-start.5
  0.6 0.0 copy-start.4
  1.3 0.0 copy-done.5
  1.3 0.0 copy-done.4
  1.3 0.0 copy-start
  1.3 1.0 %copy-done = f32[1,4,2,128,128]{4,3,2,1,0:T(8,128)S(1)} copy-done((f32[1,4,2,128,128]{4,3,2,1,0:T(8,128)S(1)}, f32[1,4,2,128,128]{4,3,2,1,0:T(8,128)}, u32[]{:S(2)}) %copy-start) | copy-done | bytes 524312
  2.4 0.0 copy-start.1
  2.4 1.0 %copy-done.1 = f32[1,2,4,128,128]{4,3,2,1,0:T(8,128)S(1)} copy-done((f32[1,2,4,128,128]{4,3,2,1,0:T(8,128)S(1)}, f32[1,2,4,128,128]{4,3,2,1,0:T(8,128)}, u32[]{:S(2)}) %copy-start.1) | copy-done | bytes 524312
  3.4 0.0 copy-start.2
  3.4 1.0 %copy-done.2 = f32[1,4,2,128,128]{4,3,2,1,0:T(8,128)S(1)} copy-done((f32[1,4,2,128,128]{4,3,2,1,0:T(8,128)S(1)}, f32[1,4,2,128,128]{4,3,2,1,0:T(8,128)}, u32[]{:S(2)}) %copy-start.2) | copy-done | bytes 524312
  4.5 0.0 copy-start.3
  4.5 0.8 %copy-done.3 = s32[1,128,128]{2,1,0:T(8,128)S(1)} copy-done((s32[1,128,128]{2,1,0:T(8,128)S(1)}, s32[1,128,128]{2,1,0:T(8,128)}, u32[]{:S(2)}) %copy-start.3) | copy-done | bytes 65560
  5.3 18.5 %window.1 = (f32[1,4,2,128,128]{4,3,2,1,0:T(8,128)S(1)}, f32[1,2,4,128,128]{4,3,2,1,0:T(8,128)S(1)}) custom-call(s32[1,4]{1,0:T(1,128)S(1)} %copy-done.4, s32[1,4]{1,0:T(1,128)S(1)} %copy-done.5, s32[1]{0:T(128)S(6)} %copy.11.wet, f32[1,4,2,128,128]{4,3,2,1,0:T(8,128)S(1)} %copy-done, f32[1,2,4,128,128]{4,3,2,1,0:T(8,128)S(1)} %copy-done.1, ...), custom_call_target="tpu_custom_call" | custom-call | tf_op jit(solution)/shard_map/window/pallas_call | solution.py:440
  23.9 0.8 %copy.12 = f32[1,4,2,128,128]{4,3,2,1,0:T(8,128)} copy(f32[1,4,2,128,128]{4,3,2,1,0:T(8,128)S(1)} %get-tuple-element.4) | data formatting | bytes 1048576
  24.7 0.8 %copy.13 = f32[1,2,4,128,128]{4,3,2,1,0:T(8,128)} copy(f32[1,2,4,128,128]{4,3,2,1,0:T(8,128)S(1)} %get-tuple-element.5) | data formatting | bytes 1048576
Async XLA Ops:
  0.6 0.7 %copy-start.5 = (s32[1,4]{1,0:T(1,128)S(1)}, s32[1,4]{1,0:T(1,128)}, u32[]{:S(2)}) copy-start(s32[1,4]{1,0:T(1,128)} %rot.1) | copy-start | bytes 52
  0.6 0.7 %copy-start.4 = (s32[1,4]{1,0:T(1,128)S(1)}, s32[1,4]{1,0:T(1,128)}, u32[]{:S(2)}) copy-start(s32[1,4]{1,0:T(1,128)} %nb.1) | copy-start | bytes 52
  1.3 1.0 %copy-start = (f32[1,4,2,128,128]{4,3,2,1,0:T(8,128)S(1)}, f32[1,4,2,128,128]{4,3,2,1,0:T(8,128)}, u32[]{:S(2)}) copy-start(f32[1,4,2,128,128]{4,3,2,1,0:T(8,128)} %state.1) | copy-start | bytes 1572868
  2.4 1.0 %copy-start.1 = (f32[1,2,4,128,128]{4,3,2,1,0:T(8,128)S(1)}, f32[1,2,4,128,128]{4,3,2,1,0:T(8,128)}, u32[]{:S(2)}) copy-start(f32[1,2,4,128,128]{4,3,2,1,0:T(8,128)} %forcing.1) | copy-start | bytes 1572868
  3.4 1.0 %copy-start.2 = (f32[1,4,2,128,128]{4,3,2,1,0:T(8,128)S(1)}, f32[1,4,2,128,128]{4,3,2,1,0:T(8,128)}, u32[]{:S(2)}) copy-start(f32[1,4,2,128,128]{4,3,2,1,0:T(8,128)} %cot.1) | copy-start | bytes 1572868
  4.5 0.8 %copy-start.3 = (s32[1,128,128]{2,1,0:T(8,128)S(1)}, s32[1,128,128]{2,1,0:T(8,128)}, u32[]{:S(2)}) copy-start(s32[1,128,128]{2,1,0:T(8,128)} %levels.1) | copy-start | bytes 196612

commit v2 on v1

--- a/solution.py
+++ b/solution.py
@@ -459,7 +459,7 @@
             pltpu.SemaphoreType.DMA((4, group + 1)), pltpu.SemaphoreType.DMA((4, group + 2)),
         ],
         compiler_params=pltpu.CompilerParams(
-            collective_id=0, has_side_effects=True, vmem_limit_bytes=32 * 1024 * 1024
+            collective_id=0, has_side_effects=True, vmem_limit_bytes=60 * 1024 * 1024
         ),
         name="window",
     )(neighbour, rotation, wet, state, forcing, cotangent, levels)

time: 25.8 us -> 23.7 us (0.919)
  local copies, waits for them, and re-layouts: 5.55 us -> 2.73 us
  Pallas kernels: 18.5 us -> 19.5 us
    unnamed x14 -> x4, local copies, waits for them, and re-layouts: 5.55 us -> 2.73 us
    pallas_call x1, Pallas kernels: 18.5 us -> 19.5 us  [shards(): pl.pallas_call(kernel, out_shape=(jax.ShapeDtypeStruct(state.shape, F32),...]
where the time goes in v2:
time: 23.7 us; the launch traced here: 23.6 us
  Pallas kernels  19.5 us (82%)
  local copies, waits for them, and re-layouts  2.73 us (12%)
  between operations  1.29 us (5%)
    pallas_call x1, Pallas kernels, shards(): pl.pallas_call(kernel, out_shape=(jax.ShapeDtypeStruct(state.shape, F32),...  19.5 us
    unnamed x4, local copies, waits for them, and re-layouts  2.73 us

profile of v2, /device:TPU:0, one launch (start us, length us, event | category | flops | bytes accessed | tf_op | source)
XLA Modules:
  0.0 23.6 jit_solution(13276267863474845856)
XLA Ops:
  1.3 19.5 %window.1 = (f32[1,4,2,128,128]{4,3,2,1,0:T(8,128)}, f32[1,2,4,128,128]{4,3,2,1,0:T(8,128)}) custom-call(s32[1,4]{1,0:T(1,128)} %nb.1, s32[1,4]{1,0:T(1,128)} %rot.1, s32[1]{0:T(128)S(6)} %copy.11.wet, f32[1,4,2,128,128]{4,3,2,1,0:T(8,128)} %state.1, f32[1,2,4,128,128]{4,3,2,1,0:T(8,128)} %forcing.1, f32[1,4,2,128,128]{4,3,2,1,0:T(8,128)} %cot.1, ...), custom_call_target="tpu_custom_call" | custom-call | tf_op jit(solution)/shard_map/window/pallas_call | solution.py:440
  20.8 0.0 copy-start
  20.8 1.9 %copy.12 = f32[1,4,2,128,128]{4,3,2,1,0:T(8,128)} copy(f32[1,4,2,128,128]{4,3,2,1,0:T(8,128)} %get-tuple-element.4) | data formatting | bytes 1048576
  22.8 0.0 copy-done
  22.8 0.8 %copy.13 = f32[1,2,4,128,128]{4,3,2,1,0:T(8,128)} copy(f32[1,2,4,128,128]{4,3,2,1,0:T(8,128)S(1)} %copy-done) | data formatting | bytes 1048576
Async XLA Ops:
  20.8 1.9 %copy-start = (f32[1,2,4,128,128]{4,3,2,1,0:T(8,128)S(1)}, f32[1,2,4,128,128]{4,3,2,1,0:T(8,128)}, u32[]{:S(2)}) copy-start(f32[1,2,4,128,128]{4,3,2,1,0:T(8,128)} %get-tuple-element.5) | copy-start | bytes 1572868

commit v3 on v2

--- a/solution.py
+++ b/solution.py
@@ -429,6 +429,22 @@
     sg_copy.wait()
 
 
+CUTS = 4
+
+
+def hand_over(sg, fg, sg_out, fg_out, sem):
+    copies = []
+    for i, (src, dst) in enumerate(((sg, sg_out), (fg, fg_out))):
+        outer, inner = src.shape[1], src.shape[2]
+        for j in range(CUTS):
+            piece = (0, j * outer // CUTS, pl.ds(j * outer % CUTS * inner // CUTS, outer * inner // CUTS))
+            copies.append(pltpu.make_async_copy(src.at[piece], dst.at[piece], sem.at[i, j]))
+    for copy in copies:
+        copy.start()
+    for copy in copies:
+        copy.wait()
+
+
 def shards(state, forcing, cotangent, neighbour, rotation, wet, levels):
     group = lax.axis_size("tile")
     anywhere = pl.BlockSpec(memory_space=pl.ANY)
@@ -437,7 +453,7 @@
     vm = lambda *shape: pltpu.VMEM(shape, F32)
     whole = lambda *shape: pltpu.VMEM(shape, jnp.int32)
     padded = vm(8, side + 2 * TOP, side)
-    return pl.pallas_call(
+    results = pl.pallas_call(
         kernel,
         out_shape=(
             jax.ShapeDtypeStruct(state.shape, F32),
@@ -463,6 +479,15 @@
         ),
         name="window",
     )(neighbour, rotation, wet, state, forcing, cotangent, levels)
+    return pl.pallas_call(
+        hand_over,
+        out_shape=tuple(jax.ShapeDtypeStruct(x.shape, F32) for x in results),
+        in_specs=[anywhere] * 2,
+        out_specs=(anywhere, anywhere),
+        scratch_shapes=[pltpu.SemaphoreType.DMA((2, CUTS))],
+        compiler_params=pltpu.CompilerParams(vmem_limit_bytes=60 * 1024 * 1024),
+        name="hand_over",
+    )(*results)
 
 
 def solution(mesh):

time: 23.7 us -> 53.9 us (2.27)
  Pallas kernels: 19.5 us -> 52.5 us
  local copies, waits for them, and re-layouts: 2.73 us -> 0 us
    pallas_call x0 -> x1, Pallas kernels: none -> 32.9 us  [shards(): pl.pallas_call(hand_over, out_shape=tuple((jax.ShapeDtypeStruct(x.shape,...]
    unnamed x4 -> x0, local copies, waits for them, and re-layouts: 2.73 us -> none
where the time goes in v3:
time: 53.9 us; the launch traced here: 53.8 us
  Pallas kernels  52.5 us (97%)
  between operations  1.29 us (2%)
    pallas_call x1, Pallas kernels, shards(): pl.pallas_call(hand_over, out_shape=tuple((jax.ShapeDtypeStruct(x.shape,...  32.9 us
    pallas_call x1, Pallas kernels, shards(): pl.pallas_call(kernel, out_shape=(jax.ShapeDtypeStruct(state.shape, F32),...  19.5 us

profile of v3, /device:TPU:0, one launch (start us, length us, event | category | flops | bytes accessed | tf_op | source)
XLA Modules:
  0.0 53.8 jit_solution(15323757881337328622)
XLA Ops:
  1.3 19.5 %window.1 = (f32[1,4,2,128,128]{4,3,2,1,0:T(8,128)}, f32[1,2,4,128,128]{4,3,2,1,0:T(8,128)}) custom-call(s32[1,4]{1,0:T(1,128)} %nb.1, s32[1,4]{1,0:T(1,128)} %rot.1, s32[1]{0:T(128)S(6)} %copy.9.wet, f32[1,4,2,128,128]{4,3,2,1,0:T(8,128)} %state.1, f32[1,2,4,128,128]{4,3,2,1,0:T(8,128)} %forcing.1, f32[1,4,2,128,128]{4,3,2,1,0:T(8,128)} %cot.1, ...), custom_call_target="tpu_custom_call" | custom-call | tf_op jit(solution)/shard_map/window/pallas_call | solution.py:456
  20.8 32.9 %hand_over.1 = (f32[1,4,2,128,128]{4,3,2,1,0:T(8,128)}, f32[1,2,4,128,128]{4,3,2,1,0:T(8,128)}) custom-call(f32[1,4,2,128,128]{4,3,2,1,0:T(8,128)} %get-tuple-element.4.sg, f32[1,2,4,128,128]{4,3,2,1,0:T(8,128)} %get-tuple-element.5.fg), custom_call_target="tpu_custom_call" | custom-call | tf_op jit(solution)/shard_map/hand_over/pallas_call | solution.py:482

commit v4 on v3

--- a/solution.py
+++ b/solution.py
@@ -9,7 +9,7 @@
 WEST, EAST, SOUTH, NORTH = 0, 1, 2, 3
 SIGN = (-1.0, 1.0, -1.0, 1.0)
 TOP = 8
-ROWS = 16
+ROWS = 32
 F32 = jnp.float32
 
 
@@ -432,17 +432,21 @@
 CUTS = 4
 
 
-def hand_over(sg, fg, sg_out, fg_out, sem):
-    copies = []
+def hand_over(sg, fg, sg_out, fg_out, held, load_sem, store_sem):
+    loads, stores = [], []
     for i, (src, dst) in enumerate(((sg, sg_out), (fg, fg_out))):
         outer, inner = src.shape[1], src.shape[2]
         for j in range(CUTS):
             piece = (0, j * outer // CUTS, pl.ds(j * outer % CUTS * inner // CUTS, outer * inner // CUTS))
-            copies.append(pltpu.make_async_copy(src.at[piece], dst.at[piece], sem.at[i, j]))
-    for copy in copies:
-        copy.start()
-    for copy in copies:
-        copy.wait()
+            loads.append(pltpu.make_async_copy(src.at[piece], held.at[i, j], load_sem.at[i, j]))
+            stores.append(pltpu.make_async_copy(held.at[i, j], dst.at[piece], store_sem.at[i, j]))
+    for load in loads:
+        load.start()
+    for load, store in zip(loads, stores):
+        load.wait()
+        store.start()
+    for store in stores:
+        store.wait()
 
 
 def shards(state, forcing, cotangent, neighbour, rotation, wet, levels):
@@ -484,7 +488,10 @@
         out_shape=tuple(jax.ShapeDtypeStruct(x.shape, F32) for x in results),
         in_specs=[anywhere] * 2,
         out_specs=(anywhere, anywhere),
-        scratch_shapes=[pltpu.SemaphoreType.DMA((2, CUTS))],
+        scratch_shapes=[
+            vm(2, CUTS, fields * depth // CUTS, side, side),
+            pltpu.SemaphoreType.DMA((2, CUTS)), pltpu.SemaphoreType.DMA((2, CUTS)),
+        ],
         compiler_params=pltpu.CompilerParams(vmem_limit_bytes=60 * 1024 * 1024),
         name="hand_over",
     )(*results)

time: 53.9 us -> 23.1 us (0.43)
  Pallas kernels: 52.5 us -> 21.6 us
    pallas_call x1, Pallas kernels: 32.9 us -> 2.09 us  [shards(): pl.pallas_call(hand_over, out_shape=tuple((jax.ShapeDtypeStruct(x.shape,...]
where the time goes in v4:
time: 23.1 us; the launch traced here: 22.9 us
  Pallas kernels  21.6 us (94%)
  between operations  1.29 us (6%)
    pallas_call x1, Pallas kernels, shards(): pl.pallas_call(kernel, out_shape=(jax.ShapeDtypeStruct(state.shape, F32),...  19.5 us
    pallas_call x1, Pallas kernels, shards(): pl.pallas_call(hand_over, out_shape=tuple((jax.ShapeDtypeStruct(x.shape,...  2.09 us

profile of v4, /device:TPU:0, one launch (start us, length us, event | category | flops | bytes accessed | tf_op | source)
XLA Modules:
  0.0 22.9 jit_solution(18167245072648336414)
XLA Ops:
  1.3 19.5 %window.1 = (f32[1,4,2,128,128]{4,3,2,1,0:T(8,128)}, f32[1,2,4,128,128]{4,3,2,1,0:T(8,128)}) custom-call(s32[1,4]{1,0:T(1,128)} %nb.1, s32[1,4]{1,0:T(1,128)} %rot.1, s32[1]{0:T(128)S(6)} %copy.9.wet, f32[1,4,2,128,128]{4,3,2,1,0:T(8,128)} %state.1, f32[1,2,4,128,128]{4,3,2,1,0:T(8,128)} %forcing.1, f32[1,4,2,128,128]{4,3,2,1,0:T(8,128)} %cot.1, ...), custom_call_target="tpu_custom_call" | custom-call | tf_op jit(solution)/shard_map/window/pallas_call | solution.py:460
  20.8 2.1 %hand_over.1 = (f32[1,4,2,128,128]{4,3,2,1,0:T(8,128)}, f32[1,2,4,128,128]{4,3,2,1,0:T(8,128)}) custom-call(f32[1,4,2,128,128]{4,3,2,1,0:T(8,128)} %get-tuple-element.4.sg, f32[1,2,4,128,128]{4,3,2,1,0:T(8,128)} %get-tuple-element.5.fg), custom_call_target="tpu_custom_call" | custom-call | tf_op jit(solution)/shard_map/hand_over/pallas_call | solution.py:486

commit v5 on v1

--- a/solution.py
+++ b/solution.py
@@ -9,7 +9,7 @@
 WEST, EAST, SOUTH, NORTH = 0, 1, 2, 3
 SIGN = (-1.0, 1.0, -1.0, 1.0)
 TOP = 8
-ROWS = 16
+ROWS = 32
 F32 = jnp.float32
 
 
@@ -153,11 +153,11 @@
 
 def kernel(
     nb, rot, wet, state, forcing, cot, levels, sg_out, fg_out,
-    st, drive, ctv, lev, mask, x0p, x1p, m2p, m1p, part, sgv, fgv, cols,
+    st, drive, ctv, lev, mask, x0p, x1p, m2p, m1p, part, cols,
     a_send, a_recv, t_send, t_recv,
     bg_send, bl_send, bu_send, bg_recv, bf_recv,
     dg_send, dl_send, du_send, dg_recv, df_recv,
-    in_sem, out_sem, send_sem, recv_sem,
+    in_sem, send_sem, recv_sem,
 ):
     group, faces = lax.axis_size("tile"), lax.axis_size("face")
     face, tile = lax.axis_index("face"), lax.axis_index("tile")
@@ -295,11 +295,9 @@
             m = ctv[p // 2, p % 2, r : r + ROWS, :] * mask[p % 2, r : r + ROWS, :]
             m2p[p, TOP + r : TOP + r + ROWS, :] = m
             if p % 2 == 0:
-                fgv[1, p // 2, r : r + ROWS, :] = m
+                fg_out[0, 1, p // 2, r : r + ROWS, :] = m
             planes.append(m)
         cols[1, r : r + ROWS, :] = pick_columns(planes)
-    fg_second = pltpu.make_async_copy(fgv.at[1], fg_out.at[0, 1], out_sem.at[0])
-    fg_second.start()
     loads[3].wait()
     for r in blocks:
         planes = step_block(x0p, drive, mask, r)
@@ -403,9 +401,7 @@
             m = m * mask[p % 2, r : r + ROWS, :]
             m1p[p, TOP + r : TOP + r + ROWS, :] = m
             if p % 2 == 0:
-                fgv[0, p // 2, r : r + ROWS, :] = m
-    fg_first = pltpu.make_async_copy(fgv.at[0], fg_out.at[0, 0], out_sem.at[1])
-    fg_first.start()
+                fg_out[0, 0, p // 2, r : r + ROWS, :] = m
     for r in blocks:
         planes = back_block(x0p, m1p, r)
         for p in range(8):
@@ -419,19 +415,15 @@
     for r in blocks:
         columns = cols[6, r : r + ROWS, :]
         for p in range(8):
-            sgv[p // 2, p % 2, r : r + ROWS, :] = part[p, r : r + ROWS, :] + put_columns(columns, p)
-    sg_copy = pltpu.make_async_copy(sgv, sg_out.at[0], out_sem.at[2])
-    sg_copy.start()
+            sg_out[0, p // 2, p % 2, r : r + ROWS, :] = part[p, r : r + ROWS, :] + put_columns(columns, p)
     for copy in copies:
         copy.wait_send()
-    fg_second.wait()
-    fg_first.wait()
-    sg_copy.wait()
 
 
 def shards(state, forcing, cotangent, neighbour, rotation, wet, levels):
     group = lax.axis_size("tile")
-    anywhere = pl.BlockSpec(memory_space=pl.ANY)
+    hbm = pl.BlockSpec(memory_space=pltpu.HBM)
+    vmem = pl.BlockSpec(memory_space=pltpu.VMEM)
     scalars = pl.BlockSpec(memory_space=pltpu.SMEM)
     fields, depth, side = state.shape[1], state.shape[2], state.shape[3]
     vm = lambda *shape: pltpu.VMEM(shape, F32)
@@ -443,26 +435,25 @@
             jax.ShapeDtypeStruct(state.shape, F32),
             jax.ShapeDtypeStruct(forcing.shape, F32),
         ),
-        in_specs=[scalars] * 3 + [anywhere] * 4,
-        out_specs=(anywhere, anywhere),
+        in_specs=[scalars] * 3 + [hbm] * 4,
+        out_specs=(vmem, vmem),
         scratch_shapes=[
             vm(fields, depth, side, side), vm(fields, side, side), vm(fields, depth, side, side),
             whole(side, side), vm(depth, side, side),
             padded, padded, padded, padded,
-            vm(8, side, side), vm(fields, depth, side, side), vm(2, fields, side, side),
-            vm(7, side, side),
+            vm(8, side, side), vm(7, side, side),
             vm(4, 8, side), vm(group + 2, 4, 8, side),
             whole(8, side), whole(group + 2, 8, side),
             vm(4, 8, side), vm(3, 8, side), vm(3, 8, side), vm(group, 4, 8, side), vm(2, 3, 8, side),
             vm(2, 8, side), vm(1, 8, side), vm(1, 8, side), vm(group, 2, 8, side), vm(2, 1, 8, side),
-            pltpu.SemaphoreType.DMA((4,)), pltpu.SemaphoreType.DMA((3,)),
+            pltpu.SemaphoreType.DMA((4,)),
             pltpu.SemaphoreType.DMA((4, group + 1)), pltpu.SemaphoreType.DMA((4, group + 2)),
         ],
         compiler_params=pltpu.CompilerParams(
             collective_id=0, has_side_effects=True, vmem_limit_bytes=32 * 1024 * 1024
         ),
         name="window",
-    )(neighbour, rotation, wet, state, forcing, cotangent, levels)
+    )(neighbour, rotation, wet, *[pltpu.with_memory_space_constraint(x, pltpu.HBM) for x in (state, forcing, cotangent, levels)])
 
 
 def solution(mesh):

time: 25.8 us -> 21.7 us (0.84)
  local copies, waits for them, and re-layouts: 5.55 us -> 1.6 us
    unnamed x14 -> x6, local copies, waits for them, and re-layouts: 5.55 us -> 1.6 us
where the time goes in v5:
time: 21.7 us; the launch traced here: 21.6 us
  Pallas kernels  18.6 us (86%)
  local copies, waits for them, and re-layouts  1.6 us (7%)
  between operations  1.34 us (6%)
    pallas_call x1, Pallas kernels, shards(): pl.pallas_call(kernel, out_shape=(jax.ShapeDtypeStruct(state.shape, F32),...  18.6 us
    unnamed x6, local copies, waits for them, and re-layouts  1.6 us

profile of v5, /device:TPU:0, one launch (start us, length us, event | category | flops | bytes accessed | tf_op | source)
XLA Modules:
  0.0 21.6 jit_solution(9873361330306587631)
XLA Ops:
  0.6 0.0 copy-start.1
  0.6 0.0 copy-start
  1.3 0.0 copy-done.1
  1.3 0.0 copy-done
  1.3 18.6 %window.1 = (f32[1,4,2,128,128]{4,3,2,1,0:T(8,128)S(1)}, f32[1,2,4,128,128]{4,3,2,1,0:T(8,128)S(1)}) custom-call(s32[1,4]{1,0:T(1,128)S(1)} %copy-done, s32[1,4]{1,0:T(1,128)S(1)} %copy-done.1, s32[1]{0:T(128)S(6)} %copy.11.wet, f32[1,4,2,128,128]{4,3,2,1,0:T(8,128)} %state.1, f32[1,2,4,128,128]{4,3,2,1,0:T(8,128)} %forcing.1, f32[1,4,2,128,128]{4,3,2,1,0:T(8,128)} %cot.1, ...), custom_call_target="tpu_custom_call" | custom-call | tf_op jit(solution)/shard_map/window/pallas_call | solution.py:432
  20.0 0.8 %copy.12 = f32[1,4,2,128,128]{4,3,2,1,0:T(8,128)} copy(f32[1,4,2,128,128]{4,3,2,1,0:T(8,128)S(1)} %get-tuple-element.4) | data formatting | bytes 1048576
  20.8 0.8 %copy.13 = f32[1,2,4,128,128]{4,3,2,1,0:T(8,128)} copy(f32[1,2,4,128,128]{4,3,2,1,0:T(8,128)S(1)} %get-tuple-element.5) | data formatting | bytes 1048576
Async XLA Ops:
  0.6 0.7 %copy-start.1 = (s32[1,4]{1,0:T(1,128)S(1)}, s32[1,4]{1,0:T(1,128)}, u32[]{:S(2)}) copy-start(s32[1,4]{1,0:T(1,128)} %rot.1) | copy-start | bytes 52
  0.6 0.7 %copy-start = (s32[1,4]{1,0:T(1,128)S(1)}, s32[1,4]{1,0:T(1,128)}, u32[]{:S(2)}) copy-start(s32[1,4]{1,0:T(1,128)} %nb.1) | copy-start | bytes 52
